TPU v7x, 128 devices: a whole 4x4x4 slice. The times are simulated.
128 devices in a mesh: bx: 16 (over z_hi, x, core), by: 8 (over z_lo, y).
Axes of the slice: x: 4, y: 4, z: 4 (z_hi: 2, z_lo: 2; z = z_hi * 2 + z_lo), core: 2. Of those that a mesh axis runs over, the one named last changes fastest.
Arguments:
- spectra: bfloat16 [16384, 10, 2, 256], P(('bx', 'by')), may hold values from -220 to 220, as said below
- band_edges: int32 [9], replicated, may hold values from 0 to 256, as said below
Outputs:
- stacked: float32 [16384, 6, 2, 8, 128], P(('bx', 'by'))
Inputs may be any that keep to these rules, and one draw needn't show every extreme that they name: `spectra`: values of moderate size for every channel, window and bin. `band_edges`: Rising; the first entry is 0, the last is 256, and each band holds at least 16 bins.
All inputs are finite; a program needn't handle non-finite values.
Results may differ from a plain program's by a relative error of at most 0.0003.
Values may be sent and summed in bfloat16 or wider, within the bound.
A program may use at most 128 MiB of HBM per device.

v0:
```python
import functools
import jax
import jax.numpy as jnp
from jax import lax
from jax.experimental import pallas as pl
from jax.experimental.pallas import tpu as pltpu
from jax.sharding import PartitionSpec as P

ROUNDS = 6
EPS = 1e-06
MESH = pl.DeviceIdType.MESH
AHEAD = 2
COMPUTE = True
COMM = True


def flip(index, bit):
    return index + bit - 2 * bit * ((index // bit) % 2)


def band_mask(edges_ref, bands, nbins):
    row = lax.broadcasted_iota(jnp.int32, (bands, nbins), 0)
    freq = lax.broadcasted_iota(jnp.int32, (bands, nbins), 1)
    low = jnp.zeros((bands, nbins), jnp.int32)
    high = jnp.zeros((bands, nbins), jnp.int32)
    for b in range(bands):
        low = jnp.where(row == b, edges_ref[b], low)
        high = jnp.where(row == b, edges_ref[b + 1], high)
    return jnp.where((freq >= low) & (freq < high), 1.0, 0.0).astype(jnp.float32)


def kernel(count, edges_ref, x_ref, acc_ref, xv, own, got, left, power, parts,
           load_sem, send_sem, recv_sem, psend_sem, precv_sem):
    channels, windows, nparts, nbins = xv.shape
    bands = power.shape[0]
    rows = nparts * channels
    bx, by = lax.axis_index("bx"), lax.axis_index("by")
    core = (flip(bx, 1), by)
    x1 = (flip(bx, 2), by)
    x3 = (flip(flip(bx, 2), 4), by)
    z1 = (bx, flip(by, 4))
    z3 = (flip(bx, 8), flip(by, 4))
    y1 = (bx, flip(by, 1))
    y2 = (bx, flip(by, 2))

    def load(c):
        return pltpu.make_async_copy(x_ref.at[:, pl.ds(c, 1)], xv.at[:, pl.ds(c, 1)], load_sem.at[c])

    for c in range(windows):
        load(c).start()

    barrier = pltpu.get_barrier_semaphore()
    ring_x = (core, x1, x3, (flip(bx, 4), by))
    ring_x = ring_x + tuple((flip(device[0], 1), by) for device in ring_x[1:])
    ring_z = (z1, z3, (flip(bx, 8), by))
    ring_y = (y1, y2, (bx, flip(flip(by, 1), 2)))
    neighbours = ring_x + ring_z + ring_y
    for device in neighbours:
        pl.semaphore_signal(barrier, inc=1, device_id=device, device_id_type=MESH)

    def copy(stream, c):
        src = {0: got.at[4, c], 1: got.at[2, c]}.get(stream, own.at[c])
        return pltpu.make_async_remote_copy(
            src_ref=src, dst_ref=got.at[stream, c], send_sem=send_sem.at[stream, c],
            recv_sem=recv_sem.at[stream, c], device_id=(z3, x3, x1, core, z1, y2)[stream], device_id_type=MESH)

    r = lax.broadcasted_iota(jnp.int32, (rows, rows), 0)
    k = lax.broadcasted_iota(jnp.int32, (rows, rows), 1)
    pick = jnp.where(k == nparts * (r % channels) + r // channels, 1.0, 0.0).astype(jnp.bfloat16)

    def prepare(c):
        load(c).wait()
        block = xv[:, c].reshape(rows, nbins)
        own[c] = jnp.dot(pick, block, preferred_element_type=jnp.float32).astype(jnp.bfloat16)

    def send(c):
        if COMM:
            for stream in (2, 4, 5, 3):
                copy(stream, c).start()

    for c in range(windows):
        prepare(c)
        if c == 0:
            pl.semaphore_wait(barrier, len(neighbours))
        if c < AHEAD:
            send(c)

    mask = band_mask(edges_ref, bands, nbins)

    def measure():
        def squares(c, total):
            v = own[c].astype(jnp.float32)
            return total + jnp.sum((v * v).reshape(rows // 8, 8, nbins), axis=0)
        bins = lax.fori_loop(0, windows, squares, jnp.zeros((8, nbins), jnp.float32))
        bins = jnp.sum(bins, axis=0, keepdims=True)
        power[...] = jnp.broadcast_to(jnp.sum(mask * bins, axis=1, keepdims=True), power.shape)

    def exchange(i):
        return pltpu.make_async_remote_copy(
            src_ref=parts.at[i], dst_ref=parts.at[len(neighbours) + i], send_sem=psend_sem.at[i],
            recv_sem=precv_sem.at[i], device_id=neighbours[i], device_id_type=MESH)

    stages = (range(7), range(7, 10), range(10, 13))

    def begin(stage):
        for i in stage:
            parts[i] = power[...]
            exchange(i).start()

    def end(stage):
        for i in stage:
            exchange(i).wait_recv()
            power[...] += parts[len(neighbours) + i]


    def build(c):
        for p in range(nparts):
            v = own[c, p * channels:(p + 1) * channels].astype(jnp.float32)
            wide = jnp.broadcast_to(v[:, None, :], (channels, bands, nbins)) * mask[None]
            left[c, :, p * nbins:(p + 1) * nbins] = wide.reshape(channels * bands, nbins).astype(jnp.bfloat16)

    def accumulate(r, c, norm=None):
        if not COMPUTE: return
        cos, sin = got[r, c, :channels], got[r, c, channels:]
        right = jnp.concatenate(
            [jnp.concatenate([cos, sin], axis=1), jnp.concatenate([-sin, cos], axis=1)], axis=0)
        product = lax.dot_general(
            left[c], right, (((1,), (1,)), ((), ())), preferred_element_type=jnp.float32)
        for p in range(2):
            value = acc_ref[:, r, p] + product[:, p * channels:(p + 1) * channels].reshape(
                channels, bands, channels)
            if norm is not None:
                value = value * norm[None]
            acc_ref[:, r, p] = value

    def wait(stream, c):
        if COMM: copy(stream, c).wait_recv()

    def start(stream, c):
        if COMM: copy(stream, c).start()

    def advance(c):
        if COMM:
            @pl.when(c + AHEAD < windows)
            def _():
                send(c + AHEAD)
        wait(2, c)
        start(1, c)
        wait(4, c)
        start(0, c)

    direct, passed = (3, 2, 4, 5), (1, 0)
    measure()
    begin(stages[0])
    if COMPUTE: build(0)
    acc_ref[...] = jnp.zeros_like(acc_ref)
    advance(0)
    if COMPUTE: build(1)
    advance(1)
    wait(3, 0)
    wait(5, 0)
    for r in direct:
        accumulate(r, 0)

    @pl.loop(2, windows)
    def _(c):
        advance(c)
        for step in range(len(stages)):
            @pl.when(c == 2 * step + 3)
            def _(step=step):
                end(stages[step])
                if step + 1 < len(stages):
                    begin(stages[step + 1])
        wait(3, c - 1)
        wait(5, c - 1)
        for r in passed:
            wait(r, c - 2)
        if COMPUTE: build(c)
        for r in direct:
            accumulate(r, c - 1)
        for r in passed:
            accumulate(r, c - 2)

    norm = 1.0 / (power[...] / (count * windows) + EPS)
    last = windows - 1
    for r in passed:
        wait(r, last - 1)
        accumulate(r, last - 1)
    wait(3, last)
    wait(5, last)
    for r in direct:
        accumulate(r, last, norm)
    for r in passed:
        wait(r, last)
    for r in passed:
        accumulate(r, last, norm)

    if COMM:
        @pl.loop(0, windows)
        def _(c):
            for stream in range(ROUNDS):
                copy(stream, c).wait_send()
    for i in range(len(neighbours)):
        exchange(i).wait_send()


def body(spectra, band_edges):
    channels, windows, parts, nbins = spectra.shape
    bands = band_edges.shape[0] - 1
    devices = lax.axis_size("bx") * lax.axis_size("by")
    rows = channels * parts
    dma = pltpu.SemaphoreType.DMA
    vmem = pltpu.VMEM
    return pl.pallas_call(
        functools.partial(kernel, channels * devices),
        out_shape=vmem((channels, ROUNDS, parts, bands, channels), jnp.float32),
        in_specs=[pl.BlockSpec(memory_space=pltpu.SMEM), pl.BlockSpec(memory_space=pl.ANY)],
        out_specs=pl.BlockSpec(memory_space=vmem),
        scratch_shapes=[
            vmem(spectra.shape, jnp.bfloat16),
            vmem((windows, rows, nbins), jnp.bfloat16),
            vmem((ROUNDS, windows, rows, nbins), jnp.bfloat16),
            vmem((windows, channels * bands, parts * nbins), jnp.bfloat16),
            vmem((bands, 128), jnp.float32),
            vmem((26, bands, 128), jnp.float32),
            dma((windows,)), dma((ROUNDS, windows)), dma((ROUNDS, windows)), dma((13,)), dma((13,)),
        ],
        compiler_params=pltpu.CompilerParams(
            collective_id=0, has_side_effects=True, vmem_limit_bytes=48 * 2**20),
        name="exchange",
    )(band_edges, spectra)


def solution(mesh):
    return jax.shard_map(
        body,
        mesh=mesh,
        in_specs=(P(("bx", "by"), None, None, None), P()),
        out_specs=P(("bx", "by"), None, None, None, None),
        check_vma=False,
    )
```

profile of v0, /device:TPU:0, one launch (start us, length us, event | category | flops | bytes accessed | tf_op | source)
XLA Modules:
  0.0 49.3 jit_solution(18080835661445713307)
XLA Ops:
  0.0 46.6 %exchange.1 = f32[128,6,2,8,128]{4,3,2,1,0:T(8,128)S(1)} custom-call(s32[9]{0:T(128)} %edges_ref.1, bf16[128,10,2,256]{3,2,1,0:T(2,128)(2,1)} %x_ref.1), custom_call_target="tpu_custom_call" | custom-call | tf_op jit(solution)/shard_map/exchange/pallas_call | solution.py:214
  46.6 2.7 %copy.4 = f32[128,6,2,8,128]{4,3,2,1,0:T(8,128)} copy(f32[128,6,2,8,128]{4,3,2,1,0:T(8,128)S(1)} %exchange.1) | data formatting | bytes 12582912
where the time goes:
time: 49.4 us; the launch traced here: 49.3 us
  Pallas kernels  46.6 us (94%)
  local copies, waits for them, and re-layouts  2.71 us (5%)
    pallas_call x1, Pallas kernels, body(): pl.pallas_call(functools.partial(kernel, channels * devices), out_shape=v...  46.6 us
    unnamed x1, local copies, waits for them, and re-layouts  2.71 us

commit v1 on v0

--- a/solution.py
+++ b/solution.py
@@ -29,7 +29,7 @@
     return jnp.where((freq >= low) & (freq < high), 1.0, 0.0).astype(jnp.float32)
 
 
-def kernel(count, edges_ref, x_ref, acc_ref, xv, own, got, left, power, parts,
+def kernel(count, edges_ref, x_ref, acc_ref, wide_ref, right_ref, norm_ref, xv, own, got, left, power, parts,
            load_sem, send_sem, recv_sem, psend_sem, precv_sem):
     channels, windows, nparts, nbins = xv.shape
     bands = power.shape[0]
@@ -46,9 +46,7 @@
     def load(c):
         return pltpu.make_async_copy(x_ref.at[:, pl.ds(c, 1)], xv.at[:, pl.ds(c, 1)], load_sem.at[c])
 
-    for c in range(windows):
-        load(c).start()
-
+    load(0).start()
     barrier = pltpu.get_barrier_semaphore()
     ring_x = (core, x1, x3, (flip(bx, 4), by))
     ring_x = ring_x + tuple((flip(device[0], 1), by) for device in ring_x[1:])
@@ -58,6 +56,10 @@
     for device in neighbours:
         pl.semaphore_signal(barrier, inc=1, device_id=device, device_id_type=MESH)
 
+    for c in range(1, windows):
+        load(c).start()
+
+
     def copy(stream, c):
         src = {0: got.at[4, c], 1: got.at[2, c]}.get(stream, own.at[c])
         return pltpu.make_async_remote_copy(
@@ -75,7 +77,7 @@
 
     def send(c):
         if COMM:
-            for stream in (2, 4, 5, 3):
+            for stream in (2, 4, 5):
                 copy(stream, c).start()
 
     for c in range(windows):
@@ -84,6 +86,8 @@
             pl.semaphore_wait(barrier, len(neighbours))
         if c < AHEAD:
             send(c)
+        if COMM:
+            copy(3, c).start()
 
     mask = band_mask(edges_ref, bands, nbins)
 
@@ -119,13 +123,17 @@
             wide = jnp.broadcast_to(v[:, None, :], (channels, bands, nbins)) * mask[None]
             left[c, :, p * nbins:(p + 1) * nbins] = wide.reshape(channels * bands, nbins).astype(jnp.bfloat16)
 
-    def accumulate(r, c, norm=None):
+    def paired(r, c):
+        cos, sin = got[r, c, :channels], got[r, c, channels:]
+        return jnp.concatenate(
+            [jnp.concatenate([cos, sin], axis=1), jnp.concatenate([-sin, cos], axis=1)], axis=0)
+
+    def accumulate(r, c, norm=None, width=1):
         if not COMPUTE: return
-        cos, sin = got[r, c, :channels], got[r, c, channels:]
-        right = jnp.concatenate(
-            [jnp.concatenate([cos, sin], axis=1), jnp.concatenate([-sin, cos], axis=1)], axis=0)
+        right = jnp.concatenate([paired(r, c + i) for i in range(width)], axis=1)
+        wide = jnp.concatenate([left[c + i] for i in range(width)], axis=1)
         product = lax.dot_general(
-            left[c], right, (((1,), (1,)), ((), ())), preferred_element_type=jnp.float32)
+            wide, right, (((1,), (1,)), ((), ())), preferred_element_type=jnp.float32)
         for p in range(2):
             value = acc_ref[:, r, p] + product[:, p * channels:(p + 1) * channels].reshape(
                 channels, bands, channels)
@@ -149,51 +157,73 @@
         wait(4, c)
         start(0, c)
 
-    direct, passed = (3, 2, 4, 5), (1, 0)
+    def builds(first, count):
+        if COMPUTE:
+            @pl.loop(first, first + count)
+            def _(c):
+                build(c)
+
+    def step(c, pair):
+        advance(c)
+        for i in range(len(stages) - 1):
+            @pl.when(c == 3 * i + 4)
+            def _(i=i):
+                end(stages[i])
+                begin(stages[i + 1])
+        if pair:
+            wait(3, 2 * c - 2)
+            wait(3, 2 * c - 1)
+        wait(5, c - 1)
+        for r in (1, 0):
+            wait(r, c - 2)
+        for r in (2, 4, 5):
+            accumulate(r, c - 1)
+        for r in (1, 0):
+            accumulate(r, c - 2)
+        if pair:
+            accumulate(3, 2 * c - 2, width=2)
+
     measure()
     begin(stages[0])
-    if COMPUTE: build(0)
+    advance(0)
     acc_ref[...] = jnp.zeros_like(acc_ref)
-    advance(0)
-    if COMPUTE: build(1)
+    builds(0, windows // 2)
     advance(1)
+    builds(windows // 2, windows - windows // 2)
     wait(3, 0)
+    wait(3, 1)
+    for r in (2, 4):
+        accumulate(r, 0)
     wait(5, 0)
-    for r in direct:
-        accumulate(r, 0)
-
-    @pl.loop(2, windows)
+    accumulate(5, 0)
+    accumulate(3, 0, width=2)
+
+    half = windows // 2 + 1
+    @pl.loop(2, half)
     def _(c):
-        advance(c)
-        for step in range(len(stages)):
-            @pl.when(c == 2 * step + 3)
-            def _(step=step):
-                end(stages[step])
-                if step + 1 < len(stages):
-                    begin(stages[step + 1])
-        wait(3, c - 1)
-        wait(5, c - 1)
-        for r in passed:
-            wait(r, c - 2)
-        if COMPUTE: build(c)
-        for r in direct:
-            accumulate(r, c - 1)
-        for r in passed:
-            accumulate(r, c - 2)
-
+        step(c, True)
+
+    @pl.loop(half, windows)
+    def _(c):
+        step(c, False)
+
+    last = windows - 1
+    end(stages[-1])
     norm = 1.0 / (power[...] / (count * windows) + EPS)
-    last = windows - 1
-    for r in passed:
+    wait(5, last)
+    for r in (1, 0):
         wait(r, last - 1)
+    for r in (2, 4, 5):
+        accumulate(r, last, norm)
+    for r in (1, 0):
         accumulate(r, last - 1)
-    wait(3, last)
-    wait(5, last)
-    for r in direct:
-        accumulate(r, last, norm)
-    for r in passed:
+    for p in range(2):
+        acc_ref[:, 3, p] = acc_ref[:, 3, p] * norm[None]
+    norm_ref[...] = norm
+    wide_ref[...] = left[last]
+    for r in (1, 0):
         wait(r, last)
-    for r in passed:
-        accumulate(r, last, norm)
+        right_ref[r] = paired(r, last)
 
     if COMM:
         @pl.loop(0, windows)
@@ -204,6 +234,25 @@
         exchange(i).wait_send()
 
 
+def finish(acc_ref, wide_ref, right_ref, norm_ref, out_ref, done, sems):
+    channels, _, parts, bands, _ = acc_ref.shape
+    count = done.shape[0]
+    early = pltpu.make_async_copy(acc_ref.at[:, count:], out_ref.at[:, count:], sems.at[count])
+    early.start()
+    norm = norm_ref[...]
+    late = []
+    for r in range(count):
+        product = lax.dot_general(
+            wide_ref[...], right_ref[r], (((1,), (1,)), ((), ())), preferred_element_type=jnp.float32)
+        for p in range(parts):
+            value = product[:, p * channels:(p + 1) * channels].reshape(channels, bands, channels)
+            done[r, :, p] = (acc_ref[:, r, p] + value) * norm[None]
+        late.append(pltpu.make_async_copy(done.at[r], out_ref.at[:, r], sems.at[r]))
+        late[-1].start()
+    for copy in (early, *late):
+        copy.wait()
+
+
 def body(spectra, band_edges):
     channels, windows, parts, nbins = spectra.shape
     bands = band_edges.shape[0] - 1
@@ -211,11 +260,14 @@
     rows = channels * parts
     dma = pltpu.SemaphoreType.DMA
     vmem = pltpu.VMEM
-    return pl.pallas_call(
+    results = pl.pallas_call(
         functools.partial(kernel, channels * devices),
-        out_shape=vmem((channels, ROUNDS, parts, bands, channels), jnp.float32),
+        out_shape=(vmem((channels, ROUNDS, parts, bands, channels), jnp.float32),
+                   vmem((channels * bands, parts * nbins), jnp.bfloat16),
+                   vmem((2, rows, parts * nbins), jnp.bfloat16),
+                   vmem((bands, 128), jnp.float32)),
         in_specs=[pl.BlockSpec(memory_space=pltpu.SMEM), pl.BlockSpec(memory_space=pl.ANY)],
-        out_specs=pl.BlockSpec(memory_space=vmem),
+        out_specs=(pl.BlockSpec(memory_space=vmem),) * 4,
         scratch_shapes=[
             vmem(spectra.shape, jnp.bfloat16),
             vmem((windows, rows, nbins), jnp.bfloat16),
@@ -226,9 +278,18 @@
             dma((windows,)), dma((ROUNDS, windows)), dma((ROUNDS, windows)), dma((13,)), dma((13,)),
         ],
         compiler_params=pltpu.CompilerParams(
-            collective_id=0, has_side_effects=True, vmem_limit_bytes=48 * 2**20),
+            collective_id=0, has_side_effects=True, vmem_limit_bytes=52 * 2**20),
         name="exchange",
     )(band_edges, spectra)
+    return pl.pallas_call(
+        finish,
+        out_shape=jax.ShapeDtypeStruct((channels, ROUNDS, parts, bands, channels), jnp.float32),
+        in_specs=[pl.BlockSpec(memory_space=vmem)] * 4,
+        out_specs=pl.BlockSpec(memory_space=pl.ANY),
+        scratch_shapes=[vmem((2, channels, parts, bands, channels), jnp.float32), dma((3,))],
+        compiler_params=pltpu.CompilerParams(vmem_limit_bytes=8 * 2**20),
+        name="finish",
+    )(*(pltpu.with_memory_space_constraint(value, vmem) for value in results))
 
 
 def solution(mesh):

time: 49.4 us -> 47.4 us (0.960)
  local copies, waits for them, and re-layouts: 2.71 us -> 0 us
  Pallas kernels: 46.6 us -> 47.3 us
    unnamed x1 -> x0, local copies, waits for them, and re-layouts: 2.71 us -> none
    pallas_call x1 -> x2, Pallas kernels: 46.6 us -> 47.3 us  [the longest x1 44.6 us: body(): pl.pallas_call(functools.partial(kernel, channels * devices), out_shape=(...]
where the time goes in v1:
time: 47.4 us; the launch traced here: 47.3 us
  Pallas kernels  47.3 us (100%)
    pallas_call x1, Pallas kernels, body(): pl.pallas_call(functools.partial(kernel, channels * devices), out_shape=(...  44.6 us
    pallas_call x1, Pallas kernels, body(): pl.pallas_call(finish, out_shape=jax.ShapeDtypeStruct((channels, ROUNDS,...  2.71 us

profile of v1, /device:TPU:0, one launch (start us, length us, event | category | flops | bytes accessed | tf_op | source)
XLA Modules:
  0.0 47.3 jit_solution(3519480772593392693)
XLA Ops:
  0.0 44.6 %exchange.1 = (f32[128,6,2,8,128]{4,3,2,1,0:T(8,128)S(1)}, bf16[1024,512]{1,0:T(8,128)(2,1)S(1)}, bf16[2,256,512]{2,1,0:T(8,128)(2,1)S(1)}, f32[8,128]{1,0:T(8,128)S(1)}) custom-call(s32[9]{0:T(128)} %edges_ref.1, bf16[128,10,2,256]{3,2,1,0:T(2,128)(2,1)} %x_ref.1), custom_call_target="tpu_custom_call" | custom-call | tf_op jit(solution)/shard_map/exchange/pallas_call | solution.py:263
  44.6 2.7 %finish.1 = f32[128,6,2,8,128]{4,3,2,1,0:T(8,128)} custom-call(f32[128,6,2,8,128]{4,3,2,1,0:T(8,128)S(1)} %get-tuple-element.9.acc_ref, bf16[1024,512]{1,0:T(8,128)(2,1)S(1)} %get-tuple-element.10.wide_ref, bf16[2,256,512]{2,1,0:T(8,128)(2,1)S(1)} %get-tuple-element.11.right_ref, f32[8,128]{1,0:T(8,128)S(1)} %get-tuple-element.12.norm_ref), custom_call_target="tpu_custom_call" | custom-call | tf_op jit(solution)/shard_map/finish/pallas_call | solution.py:284

commit v2 on v1

--- a/solution.py
+++ b/solution.py
@@ -10,6 +10,9 @@
 EPS = 1e-06
 MESH = pl.DeviceIdType.MESH
 AHEAD = 2
+EARLY = 4
+AT = (3, 6)
+START = 3
 COMPUTE = True
 COMM = True
 
@@ -29,8 +32,8 @@
     return jnp.where((freq >= low) & (freq < high), 1.0, 0.0).astype(jnp.float32)
 
 
-def kernel(count, edges_ref, x_ref, acc_ref, wide_ref, right_ref, norm_ref, xv, own, got, left, power, parts,
-           load_sem, send_sem, recv_sem, psend_sem, precv_sem):
+def kernel(count, edges_hbm, x_ref, acc_ref, wide_ref, right_ref, norm_ref, edges_ref, xv, own, got, left, power, parts,
+           edges_sem, load_sem, send_sem, recv_sem, psend_sem, precv_sem):
     channels, windows, nparts, nbins = xv.shape
     bands = power.shape[0]
     rows = nparts * channels
@@ -46,6 +49,7 @@
     def load(c):
         return pltpu.make_async_copy(x_ref.at[:, pl.ds(c, 1)], xv.at[:, pl.ds(c, 1)], load_sem.at[c])
 
+    edges = pltpu.make_async_copy(edges_hbm, edges_ref, edges_sem)
     load(0).start()
     barrier = pltpu.get_barrier_semaphore()
     ring_x = (core, x1, x3, (flip(bx, 4), by))
@@ -56,6 +60,7 @@
     for device in neighbours:
         pl.semaphore_signal(barrier, inc=1, device_id=device, device_id_type=MESH)
 
+    edges.start()
     for c in range(1, windows):
         load(c).start()
 
@@ -71,7 +76,6 @@
     pick = jnp.where(k == nparts * (r % channels) + r // channels, 1.0, 0.0).astype(jnp.bfloat16)
 
     def prepare(c):
-        load(c).wait()
         block = xv[:, c].reshape(rows, nbins)
         own[c] = jnp.dot(pick, block, preferred_element_type=jnp.float32).astype(jnp.bfloat16)
 
@@ -80,7 +84,7 @@
             for stream in (2, 4, 5):
                 copy(stream, c).start()
 
-    for c in range(windows):
+    def ready(c):
         prepare(c)
         if c == 0:
             pl.semaphore_wait(barrier, len(neighbours))
@@ -89,32 +93,32 @@
         if COMM:
             copy(3, c).start()
 
-    mask = band_mask(edges_ref, bands, nbins)
 
     def measure():
         def squares(c, total):
-            v = own[c].astype(jnp.float32)
+            v = xv[:, c].reshape(rows, nbins).astype(jnp.float32)
             return total + jnp.sum((v * v).reshape(rows // 8, 8, nbins), axis=0)
         bins = lax.fori_loop(0, windows, squares, jnp.zeros((8, nbins), jnp.float32))
         bins = jnp.sum(bins, axis=0, keepdims=True)
         power[...] = jnp.broadcast_to(jnp.sum(mask * bins, axis=1, keepdims=True), power.shape)
 
+    stages = (range(7), range(7, 10), range(10, 13))
+
     def exchange(i):
+        stage = [i in s for s in stages].index(True)
         return pltpu.make_async_remote_copy(
-            src_ref=parts.at[i], dst_ref=parts.at[len(neighbours) + i], send_sem=psend_sem.at[i],
+            src_ref=parts.at[stage], dst_ref=parts.at[len(stages) + i], send_sem=psend_sem.at[i],
             recv_sem=precv_sem.at[i], device_id=neighbours[i], device_id_type=MESH)
 
-    stages = (range(7), range(7, 10), range(10, 13))
-
     def begin(stage):
+        parts[stages.index(stage)] = power[...]
         for i in stage:
-            parts[i] = power[...]
             exchange(i).start()
 
     def end(stage):
         for i in stage:
             exchange(i).wait_recv()
-            power[...] += parts[len(neighbours) + i]
+            power[...] += parts[len(stages) + i]
 
 
     def build(c):
@@ -128,15 +132,16 @@
         return jnp.concatenate(
             [jnp.concatenate([cos, sin], axis=1), jnp.concatenate([-sin, cos], axis=1)], axis=0)
 
-    def accumulate(r, c, norm=None, width=1):
+    def accumulate(r, c, norm=None, width=1, first=False):
         if not COMPUTE: return
         right = jnp.concatenate([paired(r, c + i) for i in range(width)], axis=1)
         wide = jnp.concatenate([left[c + i] for i in range(width)], axis=1)
         product = lax.dot_general(
             wide, right, (((1,), (1,)), ((), ())), preferred_element_type=jnp.float32)
         for p in range(2):
-            value = acc_ref[:, r, p] + product[:, p * channels:(p + 1) * channels].reshape(
-                channels, bands, channels)
+            value = product[:, p * channels:(p + 1) * channels].reshape(channels, bands, channels)
+            if not first:
+                value = acc_ref[:, r, p] + value
             if norm is not None:
                 value = value * norm[None]
             acc_ref[:, r, p] = value
@@ -164,15 +169,16 @@
                 build(c)
 
     def step(c, pair):
-        advance(c)
         for i in range(len(stages) - 1):
-            @pl.when(c == 3 * i + 4)
+            @pl.when(c == AT[i])
             def _(i=i):
                 end(stages[i])
                 begin(stages[i + 1])
+        advance(c)
         if pair:
-            wait(3, 2 * c - 2)
-            wait(3, 2 * c - 1)
+            at = 2 * c - 2 * START
+            wait(3, at)
+            wait(3, at + 1)
         wait(5, c - 1)
         for r in (1, 0):
             wait(r, c - 2)
@@ -181,25 +187,40 @@
         for r in (1, 0):
             accumulate(r, c - 2)
         if pair:
-            accumulate(3, 2 * c - 2, width=2)
-
+            accumulate(3, at, width=2)
+
+    load(0).wait()
+    ready(0)
+    edges.wait()
+    mask = band_mask(edges_ref, bands, nbins)
+    for c in range(1, windows):
+        load(c).wait()
     measure()
     begin(stages[0])
+    for c in range(1, EARLY):
+        ready(c)
     advance(0)
-    acc_ref[...] = jnp.zeros_like(acc_ref)
-    builds(0, windows // 2)
+    for c in range(EARLY, windows):
+        ready(c)
+    builds(0, 4)
     advance(1)
-    builds(windows // 2, windows - windows // 2)
-    wait(3, 0)
-    wait(3, 1)
-    for r in (2, 4):
-        accumulate(r, 0)
     wait(5, 0)
-    accumulate(5, 0)
-    accumulate(3, 0, width=2)
-
-    half = windows // 2 + 1
-    @pl.loop(2, half)
+    for r in (2, 4, 5):
+        accumulate(r, 0, first=True)
+    acc_ref[:, 3] = jnp.zeros_like(acc_ref[:, 3])
+    builds(4, 2)
+    advance(2)
+    wait(5, 1)
+    for r in (1, 0):
+        wait(r, 0)
+    for r in (2, 4, 5):
+        accumulate(r, 1)
+    for r in (1, 0):
+        accumulate(r, 0, first=True)
+    builds(6, windows - 6)
+
+    half = START + windows // 2
+    @pl.loop(START, half)
     def _(c):
         step(c, True)
 
@@ -266,16 +287,17 @@
                    vmem((channels * bands, parts * nbins), jnp.bfloat16),
                    vmem((2, rows, parts * nbins), jnp.bfloat16),
                    vmem((bands, 128), jnp.float32)),
-        in_specs=[pl.BlockSpec(memory_space=pltpu.SMEM), pl.BlockSpec(memory_space=pl.ANY)],
+        in_specs=[pl.BlockSpec(memory_space=pl.ANY), pl.BlockSpec(memory_space=pl.ANY)],
         out_specs=(pl.BlockSpec(memory_space=vmem),) * 4,
         scratch_shapes=[
+            pltpu.SMEM(band_edges.shape, jnp.int32),
             vmem(spectra.shape, jnp.bfloat16),
             vmem((windows, rows, nbins), jnp.bfloat16),
             vmem((ROUNDS, windows, rows, nbins), jnp.bfloat16),
             vmem((windows, channels * bands, parts * nbins), jnp.bfloat16),
             vmem((bands, 128), jnp.float32),
-            vmem((26, bands, 128), jnp.float32),
-            dma((windows,)), dma((ROUNDS, windows)), dma((ROUNDS, windows)), dma((13,)), dma((13,)),
+            vmem((16, bands, 128), jnp.float32),
+            dma(()), dma((windows,)), dma((ROUNDS, windows)), dma((ROUNDS, windows)), dma((13,)), dma((13,)),
         ],
         compiler_params=pltpu.CompilerParams(
             collective_id=0, has_side_effects=True, vmem_limit_bytes=52 * 2**20),

time: 47.4 us -> 46.6 us (0.983)
  Pallas kernels: 47.3 us -> 46.5 us
    pallas_call x1, Pallas kernels: 44.6 us -> 43.8 us  [body(): pl.pallas_call(functools.partial(kernel, channels * devices), out_shape=(...]
where the time goes in v2:
time: 46.6 us; the launch traced here: 46.5 us
  Pallas kernels  46.5 us (100%)
    pallas_call x1, Pallas kernels, body(): pl.pallas_call(functools.partial(kernel, channels * devices), out_shape=(...  43.8 us
    pallas_call x1, Pallas kernels, body(): pl.pallas_call(finish, out_shape=jax.ShapeDtypeStruct((channels, ROUNDS,...  2.71 us

profile of v2, /device:TPU:0, one launch (start us, length us, event | category | flops | bytes accessed | tf_op | source)
XLA Modules:
  0.0 46.5 jit_solution(128990343066692577)
XLA Ops:
  0.0 43.8 %exchange.1 = (f32[128,6,2,8,128]{4,3,2,1,0:T(8,128)S(1)}, bf16[1024,512]{1,0:T(8,128)(2,1)S(1)}, bf16[2,256,512]{2,1,0:T(8,128)(2,1)S(1)}, f32[8,128]{1,0:T(8,128)S(1)}) custom-call(s32[9]{0:T(128)} %edges_hbm.1, bf16[128,10,2,256]{3,2,1,0:T(2,128)(2,1)} %x_ref.1), custom_call_target="tpu_custom_call" | custom-call | tf_op jit(solution)/shard_map/exchange/pallas_call | solution.py:284
  43.8 2.7 %finish.1 = f32[128,6,2,8,128]{4,3,2,1,0:T(8,128)} custom-call(f32[128,6,2,8,128]{4,3,2,1,0:T(8,128)S(1)} %get-tuple-element.9.acc_ref, bf16[1024,512]{1,0:T(8,128)(2,1)S(1)} %get-tuple-element.10.wide_ref, bf16[2,256,512]{2,1,0:T(8,128)(2,1)S(1)} %get-tuple-element.11.right_ref, f32[8,128]{1,0:T(8,128)S(1)} %get-tuple-element.12.norm_ref), custom_call_target="tpu_custom_call" | custom-call | tf_op jit(solution)/shard_map/finish/pallas_call | solution.py:306

commit v3 on v2

--- a/solution.py
+++ b/solution.py
@@ -153,14 +153,14 @@
         if COMM: copy(stream, c).start()
 
     def advance(c):
+        wait(4, c)
+        start(0, c)
+        wait(2, c)
+        start(1, c)
         if COMM:
             @pl.when(c + AHEAD < windows)
             def _():
                 send(c + AHEAD)
-        wait(2, c)
-        start(1, c)
-        wait(4, c)
-        start(0, c)
 
     def builds(first, count):
         if COMPUTE:

time: 46.6 us -> 46.1 us (0.989)
  Pallas kernels: 46.5 us -> 45.9 us
    pallas_call x1, Pallas kernels: 43.8 us -> 43.2 us  [body(): pl.pallas_call(functools.partial(kernel, channels * devices), out_shape=(...]
where the time goes in v3:
time: 46.1 us; the launch traced here: 45.9 us
  Pallas kernels  45.9 us (100%)
    pallas_call x1, Pallas kernels, body(): pl.pallas_call(functools.partial(kernel, channels * devices), out_shape=(...  43.2 us
    pallas_call x1, Pallas kernels, body(): pl.pallas_call(finish, out_shape=jax.ShapeDtypeStruct((channels, ROUNDS,...  2.71 us

profile of v3, /device:TPU:0, one launch (start us, length us, event | category | flops | bytes accessed | tf_op | source)
XLA Modules:
  0.0 45.9 jit_solution(6908886311403925381)
XLA Ops:
  0.0 43.2 %exchange.1 = (f32[128,6,2,8,128]{4,3,2,1,0:T(8,128)S(1)}, bf16[1024,512]{1,0:T(8,128)(2,1)S(1)}, bf16[2,256,512]{2,1,0:T(8,128)(2,1)S(1)}, f32[8,128]{1,0:T(8,128)S(1)}) custom-call(s32[9]{0:T(128)} %edges_hbm.1, bf16[128,10,2,256]{3,2,1,0:T(2,128)(2,1)} %x_ref.1), custom_call_target="tpu_custom_call" | custom-call | tf_op jit(solution)/shard_map/exchange/pallas_call | solution.py:284
  43.2 2.7 %finish.1 = f32[128,6,2,8,128]{4,3,2,1,0:T(8,128)} custom-call(f32[128,6,2,8,128]{4,3,2,1,0:T(8,128)S(1)} %get-tuple-element.9.acc_ref, bf16[1024,512]{1,0:T(8,128)(2,1)S(1)} %get-tuple-element.10.wide_ref, bf16[2,256,512]{2,1,0:T(8,128)(2,1)S(1)} %get-tuple-element.11.right_ref, f32[8,128]{1,0:T(8,128)S(1)} %get-tuple-element.12.norm_ref), custom_call_target="tpu_custom_call" | custom-call | tf_op jit(solution)/shard_map/finish/pallas_call | solution.py:306

commit v4 on v3

--- a/solution.py
+++ b/solution.py
@@ -193,11 +193,13 @@
     ready(0)
     edges.wait()
     mask = band_mask(edges_ref, bands, nbins)
-    for c in range(1, windows):
+    load(1).wait()
+    ready(1)
+    for c in range(2, windows):
         load(c).wait()
     measure()
     begin(stages[0])
-    for c in range(1, EARLY):
+    for c in range(2, EARLY):
         ready(c)
     advance(0)
     for c in range(EARLY, windows):

time: 46.1 us -> 46.1 us (level)
  no operation moved by 1% of the time
where the time goes in v4:
time: 46.1 us; the launch traced here: 45.9 us
  Pallas kernels  45.9 us (100%)
    pallas_call x1, Pallas kernels, body(): pl.pallas_call(functools.partial(kernel, channels * devices), out_shape=(...  43.2 us
    pallas_call x1, Pallas kernels, body(): pl.pallas_call(finish, out_shape=jax.ShapeDtypeStruct((channels, ROUNDS,...  2.71 us

profile of v4, /device:TPU:0, one launch (start us, length us, event | category | flops | bytes accessed | tf_op | source)
XLA Modules:
  0.0 45.9 jit_solution(1261097122451575661)
XLA Ops:
  0.0 43.2 %exchange.1 = (f32[128,6,2,8,128]{4,3,2,1,0:T(8,128)S(1)}, bf16[1024,512]{1,0:T(8,128)(2,1)S(1)}, bf16[2,256,512]{2,1,0:T(8,128)(2,1)S(1)}, f32[8,128]{1,0:T(8,128)S(1)}) custom-call(s32[9]{0:T(128)} %edges_hbm.1, bf16[128,10,2,256]{3,2,1,0:T(2,128)(2,1)} %x_ref.1), custom_call_target="tpu_custom_call" | custom-call | tf_op jit(solution)/shard_map/exchange/pallas_call | solution.py:286
  43.2 2.7 %finish.1 = f32[128,6,2,8,128]{4,3,2,1,0:T(8,128)} custom-call(f32[128,6,2,8,128]{4,3,2,1,0:T(8,128)S(1)} %get-tuple-element.9.acc_ref, bf16[1024,512]{1,0:T(8,128)(2,1)S(1)} %get-tuple-element.10.wide_ref, bf16[2,256,512]{2,1,0:T(8,128)(2,1)S(1)} %get-tuple-element.11.right_ref, f32[8,128]{1,0:T(8,128)S(1)} %get-tuple-element.12.norm_ref), custom_call_target="tpu_custom_call" | custom-call | tf_op jit(solution)/shard_map/finish/pallas_call | solution.py:308

commit v5 on v4

--- a/solution.py
+++ b/solution.py
@@ -9,8 +9,8 @@
 ROUNDS = 6
 EPS = 1e-06
 MESH = pl.DeviceIdType.MESH
-AHEAD = 2
-EARLY = 4
+AHEAD = 3
+EARLY = 5
 AT = (3, 6)
 START = 3
 COMPUTE = True

time: 46.1 us -> 46.1 us (level)
  no operation moved by 1% of the time
where the time goes in v5:
time: 46.1 us; the launch traced here: 45.9 us
  Pallas kernels  45.9 us (100%)
    pallas_call x1, Pallas kernels, body(): pl.pallas_call(functools.partial(kernel, channels * devices), out_shape=(...  43.2 us
    pallas_call x1, Pallas kernels, body(): pl.pallas_call(finish, out_shape=jax.ShapeDtypeStruct((channels, ROUNDS,...  2.71 us

profile of v5, /device:TPU:0, one launch (start us, length us, event | category | flops | bytes accessed | tf_op | source)
XLA Modules:
  0.0 45.9 jit_solution(10500841928025575330)
XLA Ops:
  0.0 43.2 %exchange.1 = (f32[128,6,2,8,128]{4,3,2,1,0:T(8,128)S(1)}, bf16[1024,512]{1,0:T(8,128)(2,1)S(1)}, bf16[2,256,512]{2,1,0:T(8,128)(2,1)S(1)}, f32[8,128]{1,0:T(8,128)S(1)}) custom-call(s32[9]{0:T(128)} %edges_hbm.1, bf16[128,10,2,256]{3,2,1,0:T(2,128)(2,1)} %x_ref.1), custom_call_target="tpu_custom_call" | custom-call | tf_op jit(solution)/shard_map/exchange/pallas_call | solution.py:286
  43.2 2.7 %finish.1 = f32[128,6,2,8,128]{4,3,2,1,0:T(8,128)} custom-call(f32[128,6,2,8,128]{4,3,2,1,0:T(8,128)S(1)} %get-tuple-element.9.acc_ref, bf16[1024,512]{1,0:T(8,128)(2,1)S(1)} %get-tuple-element.10.wide_ref, bf16[2,256,512]{2,1,0:T(8,128)(2,1)S(1)} %get-tuple-element.11.right_ref, f32[8,128]{1,0:T(8,128)S(1)} %get-tuple-element.12.norm_ref), custom_call_target="tpu_custom_call" | custom-call | tf_op jit(solution)/shard_map/finish/pallas_call | solution.py:308
